TPU v7x, 128 devices: a whole 4x4x4 slice. The times are simulated.
128 devices in a mesh: dp: 8 (over y_lo, z), ctx: 16 (over y_hi, x, core).
Axes of the slice: x: 4, y: 4 (y_hi: 2, y_lo: 2; y = y_hi * 2 + y_lo), z: 4, core: 2. Of those that a mesh axis runs over, the one named last changes fastest.
Arguments:
- tokens: bfloat16 [16384, 1024], P(('dp', 'ctx')), may hold values from -6 to 6
- cotangent: bfloat16 [16384, 1024], P(('dp', 'ctx')), may hold values from -6 to 6
- block_order: int32 [16], replicated, may hold values from 0 to 15, each once
- routes: int32 [16384, 8], P(('dp', 'ctx')), may hold values from 0 to 31, all different within a row; in each aligned block of 128 rows (0 to 127, 128 to 255, ...) at most 48 rows name the same one
- norm_one: bfloat16 [1024], P(('dp', 'ctx')), may hold values from 0.099609375 to 1.8984375
- w_query: bfloat16 [1024, 1024], P(('dp', 'ctx')), may hold values from -0.1875 to 0.1875
- w_key: bfloat16 [1024, 512], P(('dp', 'ctx')), may hold values from -0.1875 to 0.1875
- w_value: bfloat16 [1024, 512], P(('dp', 'ctx')), may hold values from -0.1875 to 0.1875
- w_out: bfloat16 [1024, 1024], P(('dp', 'ctx')), may hold values from -3 to 3
- norm_two: bfloat16 [1024], P(('dp', 'ctx')), may hold values from 0.099609375 to 1.8984375
- w_router: bfloat16 [1024, 32], P(('dp', 'ctx')), may hold values from -0.09375 to 0.09375
- expert_in: bfloat16 [32, 1024, 1024], P('ctx', 'dp'), may hold values from -0.1875 to 0.1875
- expert_out: bfloat16 [32, 512, 1024], P('ctx', None, 'dp'), may hold values from -1 to 1
Outputs:
- output: float32 [16384, 1024], P(('dp', 'ctx'))
- input_grad: float32 [16384, 1024], P(('dp', 'ctx'))
- grad_norm_one: float32 [1024], P(('dp', 'ctx'))
- grad_w_query: float32 [1024, 1024], P(('dp', 'ctx'))
- grad_w_key: float32 [1024, 512], P(('dp', 'ctx'))
- grad_w_value: float32 [1024, 512], P(('dp', 'ctx'))
- grad_w_out: float32 [1024, 1024], P(('dp', 'ctx'))
- grad_norm_two: float32 [1024], P(('dp', 'ctx'))
- grad_w_router: float32 [1024, 32], P(('dp', 'ctx'))
- grad_expert_in: float32 [32, 1024, 1024], P('ctx', 'dp')
- grad_expert_out: float32 [32, 512, 1024], P('ctx', None, 'dp')
Inputs may be any that keep to these rules, and one draw needn't show every extreme that they name: `routes`: each row names 8 different experts; the rows of one device name any expert at most 48 times, a bound that some block reaches. A permutation; ctx index c holds, in this order, blocks block_order[c] and 31 - block_order[c] of its sequence's 2 * 16 blocks.
All inputs are finite; a program needn't handle non-finite values.
Results may differ from a plain program's by a relative error of at most 0.024.
Values may be sent and summed in bfloat16 or wider, within the bound.
A program may use at most 128 MiB of HBM per device.

v0:
```python
import functools
import math

import jax
import jax.numpy as jnp
import numpy as np
from jax import lax
from jax.experimental import pallas as pl
from jax.experimental.pallas import tpu as pltpu
from jax.sharding import Mesh
from jax.sharding import PartitionSpec as P

D = 1024
HEADS = 16
KV_HEADS = 8
HEAD_DIM = 64
EXPERTS = 32
FF = 512
TOP = 8
MOST = 48
ROWS = 128
SEQ = 2048
BLOCK = 64
AXES = ("ylo", "z", "yhi", "x", "core")
DP = ("ylo", "z")
CTX = ("yhi", "x", "core")
N_DP = 8
N_CTX = 16
EXTRA = 128
MESH_ID = pl.DeviceIdType.MESH
ANY = pl.BlockSpec(memory_space=pl.ANY)
VMEM = pl.BlockSpec(memory_space=pltpu.VMEM)
SMEM = pl.BlockSpec(memory_space=pltpu.SMEM)
DMA = pltpu.SemaphoreType.DMA
bf16 = jnp.bfloat16
f32 = jnp.float32
epsilon = 1e-06


def dot(a, b):
    return jnp.dot(a, b, preferred_element_type=f32)


def dot_last(a, b):
    return lax.dot_general(a, b, (((1,), (1,)), ((), ())), preferred_element_type=f32)


def dot_first(a, b):
    return lax.dot_general(a, b, (((0,), (0,)), ((), ())), preferred_element_type=f32)


def my_place():
    return tuple(lax.axis_index(a) for a in AXES)


def device_at(dp, ctx):
    return (
        lax.div(dp, 4),
        lax.rem(dp, 4),
        lax.div(ctx, 8),
        lax.rem(lax.div(ctx, 2), 4),
        lax.rem(ctx, 2),
    )


def beside(place, dy, dx):
    ylo, z, yhi, x, core = place
    return (ylo, z, lax.rem(yhi + dy, 2), lax.rem(x + dx, 4), core)


def ctx_of(place):
    return place[2] * 8 + place[3] * 2 + place[4]


def dp_of(place):
    return place[0] * 4 + place[1]


def sibling_of(place):
    return place[:4] + (1 - place[4],)


def remote(src, dst, send, recv, device):
    return pltpu.make_async_remote_copy(
        src_ref=src, dst_ref=dst, send_sem=send, recv_sem=recv, device_id=device, device_id_type=MESH_ID
    )


def greet(devices):
    barrier = pltpu.get_barrier_semaphore()
    for device in devices:
        pl.semaphore_signal(barrier, inc=1, device_id=device, device_id_type=MESH_ID)
    return barrier


class RowGather:
    scratch = [DMA, DMA((9,)), DMA((9,)), DMA((10,)), DMA((10,))]
    links = [(1, 0), (0, 1), (0, 3), (0, 1), (0, 3), (0, 1), (0, 3), (0, 1), (0, 3)]
    held = [(0, 0), (0, 0), (0, 0), (1, 0), (1, 0), (0, 3), (0, 1), (1, 3), (1, 1)]
    parts = [None, None, None, None, None, 0, 1, 0, 1]
    after = {0: (3, 4), 1: (5,), 2: (6,), 3: (7,), 4: (8,)}

    def __init__(self, place, x_ref, view, half, local, send, recv, fsend, frecv):
        sibling = sibling_of(place)

        def piece(dy, dx, part):
            ref = view(beside(place, dy, dx))
            return ref if part is None else ref.at[pl.ds(part * half, half)]

        self.own = pltpu.make_async_copy(x_ref, view(place), local)
        self.out, self.landed, self.passed = [], [], []
        for n, ((ly, lx), (hy, hx), part) in enumerate(zip(self.links, self.held, self.parts)):
            source = x_ref if n < 3 else piece(hy, hx, part)
            self.out.append(
                remote(source, piece(hy, hx, part), send.at[n], recv.at[n], beside(place, ly, lx))
            )
            here = piece((hy + ly) % 2, (hx + 4 - lx) % 4, part)
            self.landed.append(remote(here, here, send.at[n], recv.at[n], beside(place, ly, lx)))
            self.passed.append(remote(here, here, fsend.at[n], frecv.at[n], sibling))
        self.passed.append(remote(x_ref, view(place), fsend.at[9], frecv.at[9], sibling))
        self.back = []
        for n in range(9):
            (ly, lx), (hy, hx), part = self.links[n], self.held[n], self.parts[n]
            ref = view(sibling_of(beside(place, (hy + ly) % 2, (hx + 4 - lx) % 4)))
            ref = ref if part is None else ref.at[pl.ds(part * half, half)]
            self.back.append(remote(ref, ref, fsend.at[n], frecv.at[n], sibling))
        ref = view(sibling)
        self.back.append(remote(ref, ref, fsend.at[9], frecv.at[9], sibling))

    def start(self):
        for n in range(3):
            self.out[n].start()
        self.passed[9].start()
        self.own.start()

    def step(self, n):
        self.landed[n].wait_recv()
        for m in self.after.get(n, ()):
            self.out[m].start()
        self.passed[n].start()

    def pass_on(self):
        for n in range(9):
            self.step(n)

    def finish(self):
        self.own.wait()
        for n in range(10):
            self.back[n].wait_recv()
        for copy in self.out + self.passed:
            copy.wait_send()


def chip_neighbours(place):
    return [beside(place, 1, 0), beside(place, 0, 1), beside(place, 0, 3), sibling_of(place)]


SPREAD = [(1, 2), (0, 2), (1, 1), (1, 3), (0, 1), (0, 3), (1, 0), (0, 0)]


class RowScatter:
    @staticmethod
    def scratch(rows, width):
        return [
            pltpu.VMEM((8, rows, width), bf16),
            pltpu.VMEM((8, rows, width), bf16),
            pltpu.VMEM((4, rows // 2, width), bf16),
            pltpu.VMEM((4, rows, width), bf16),
            pltpu.VMEM((rows, width), bf16),
            DMA((8,)),
            DMA((8,)),
            DMA((8,)),
            DMA((9,)),
            DMA((9,)),
        ]

    def __init__(self, place, part, own, other, halves, wholes, last, own_sem, fsend, frecv, send, recv):
        self.own, self.other, self.halves, self.wholes, self.last = own, other, halves, wholes, last
        core = place[4]
        half = own.shape[1] // 2
        self.half = half
        self.mine, self.cross = [], []
        for n, (dy, dx) in enumerate(SPREAD):
            chip = lax.div(ctx_of(beside(place, dy, dx)), 2)
            self.mine.append(pltpu.make_async_copy(part(chip, core), own.at[n], own_sem.at[n]))
            self.cross.append(
                remote(part(chip, 1 - core), other.at[n], fsend.at[n], frecv.at[n], sibling_of(place))
            )
        right, left = beside(place, 0, 1), beside(place, 0, 3)
        self.out = []
        for n, (source, target, device) in enumerate(
            [
                (own.at[0, pl.ds(0, half)], halves.at[0], right),
                (own.at[0, pl.ds(half, half)], halves.at[1], left),
                (own.at[1, pl.ds(0, half)], halves.at[2], right),
                (own.at[1, pl.ds(half, half)], halves.at[3], left),
                (own.at[2], wholes.at[0], right),
                (own.at[3], wholes.at[1], left),
                (own.at[4], wholes.at[2], right),
                (own.at[5], wholes.at[3], left),
                (own.at[6], last, beside(place, 1, 0)),
            ]
        ):
            self.out.append(remote(source, target, send.at[n], recv.at[n], device))

    def start(self, n):
        self.cross[n].start()
        self.mine[n].start()

    def release(self):
        for n in range(8):
            self.cross[n].wait_send()

    def join(self, n):
        self.mine[n].wait()
        self.cross[n].wait_recv()
        return self.own[n].astype(f32) + self.other[n].astype(f32)

    def step(self, n):
        if n < 2:
            self.own[n] = self.join(n).astype(bf16)
            self.out[2 * n].start()
            self.out[2 * n + 1].start()
        elif n < 6:
            total = self.join(n)
            half = self.half
            side = pl.ds(0 if n % 2 == 0 else half, half)
            self.out[n - 2].wait_recv()
            self.own[n] = total.astype(bf16)
            first = total[:half] if n % 2 == 0 else total[half:]
            self.own[n, side] = (first + self.halves[n - 2].astype(f32)).astype(bf16)
            self.out[n + 2].start()
        elif n == 6:
            total = self.join(6)
            for m in (0, 1):
                self.out[4 + m].wait_recv()
                total = total + self.wholes[m].astype(f32)
            self.own[6] = total.astype(bf16)
            self.out[8].start()
        else:
            total = self.join(7)
            for m in (2, 3):
                self.out[4 + m].wait_recv()
                total = total + self.wholes[m].astype(f32)
            self.out[8].wait_recv()
            return total + self.last[...].astype(f32)

    def finish(self):
        for copy in self.out:
            copy.wait_send()


def entry_kernel(
    x_ref, q_ref, k_ref, v_ref, small_ref, o_ref, routes_ref, x_out, w_out, o_out, m_out,
    w_pack, o_pad, o_other, o_mid, m_pack, *sems,
):
    row_sems, o_sems, m_sems, rest = sems[:5], sems[5:10], sems[10:15], sems[15:]
    wlocal, wsend, wrecv, psend, precv, xsend, xrecv, osend, orecv = rest
    place = my_place()
    core = place[4]
    dp, ctx = dp_of(place), ctx_of(place)
    barrier = greet(
        [device_at(dp, lax.rem(ctx + k, N_CTX)) for k in range(1, N_CTX)]
        + [device_at(lax.rem(dp + k, N_DP), ctx) for k in range(1, N_DP)]
    )
    pl.semaphore_wait(barrier, 22)
    rows = RowGather(place, x_ref, lambda p: x_out.at[ctx_of(p)], x_ref.shape[0] // 2, *row_sems)
    rows.start()

    out = o_ref[...].astype(f32)
    empty = jnp.zeros_like(out)
    out = jnp.where(core == 0, jnp.concatenate([out, empty], 0), jnp.concatenate([empty, out], 0))
    for s in range(2):
        o_pad[s] = out[:, s * 512 : (s + 1) * 512].astype(bf16)
    swap = remote(o_pad.at[1 - core], o_other, xsend, xrecv, sibling_of(place))
    swap.start()
    query, key, value = (r[...].astype(f32) for r in (q_ref, k_ref, v_ref))
    small = small_ref[...].astype(f32)
    for h in range(HEADS):
        at, pair = slice(h * 64, h * 64 + 64), slice(h // 2 * 64, h // 2 * 64 + 64)
        top = jnp.concatenate([query[:, at], key[:, pair]], axis=1)
        low = jnp.concatenate([value[:, pair], small], axis=1)
        w_pack[h] = jnp.concatenate([top, low], axis=0).astype(bf16)
    first, second, third = [], [], []
    for k in range(1, N_CTX):
        to = lax.rem(ctx + k, N_CTX)
        first.append(
            remote(w_pack.at[to], w_out.at[dp, ctx], wsend.at[k], wrecv.at[k], device_at(dp, to))
        )
    for k in range(1, N_DP):
        device = device_at(lax.rem(dp + k, N_DP), ctx)
        third.append(remote(o_mid.at[dp], o_mid.at[dp], osend.at[k], orecv.at[k], device))
        second.append(remote(w_out.at[dp], w_out.at[dp], psend.at[k], precv.at[k], device))
    for copy in first:
        copy.start()
    own = pltpu.make_async_copy(w_pack.at[ctx], w_out.at[dp, ctx], wlocal)
    own.start()
    swap.wait_recv()
    o_mid[dp] = o_pad[core] + o_other[...]
    for copy in third:
        copy.start()
    routes = routes_ref[...]
    lane = lax.broadcasted_iota(jnp.int32, (ROWS, EXTRA), 1) - 64
    member = jnp.zeros((ROWS, EXTRA), f32)
    for k in range(TOP):
        member = jnp.where(lane == routes[:, k : k + 1], 1.0, member)
    m_pack[...] = member.astype(bf16)
    members = RowGather(place, m_pack, lambda p: m_out.at[ctx_of(p)], ROWS // 2, *m_sems)
    members.start()
    own.wait()
    for copy in first:
        copy.wait_recv()
    for copy in second:
        copy.start()
    for copy in third:
        copy.wait_recv()

    def o_view(p):
        return o_out.at[:, p[2] * 4 + p[3], :, pl.ds(pl.multiple_of(p[4] * 512, 512), 512)]

    outs = RowGather(place, o_mid, o_view, 4, *o_sems)
    outs.start()
    for n in range(5):
        rows.step(n)
    for n in range(9):
        members.step(n)
    for n in range(3):
        outs.step(n)
    for n in range(5, 9):
        rows.step(n)
    for n in range(3, 9):
        outs.step(n)
    rows.finish()
    members.finish()
    outs.finish()
    for copy in second:
        copy.wait_recv()
    swap.wait_send()
    for copy in first + second + third:
        copy.wait_send()


def entry(x, query, key, value, small, out, routes, number):
    return pl.pallas_call(
        entry_kernel,
        out_shape=(
            jax.ShapeDtypeStruct((N_CTX,) + x.shape, bf16),
            jax.ShapeDtypeStruct((N_DP, N_CTX, 16, 128), bf16),
            jax.ShapeDtypeStruct((N_DP, 8, 16, D), bf16),
            jax.ShapeDtypeStruct((N_CTX, ROWS, EXTRA), bf16),
        ),
        in_specs=[ANY] + [VMEM] * 6,
        out_specs=(ANY,) * 4,
        scratch_shapes=[
            pltpu.VMEM((N_CTX, 16, 128), bf16),
            pltpu.VMEM((2, 16, 512), bf16),
            pltpu.VMEM((16, 512), bf16),
            pltpu.VMEM((N_DP, 16, 512), bf16),
            pltpu.VMEM((ROWS, EXTRA), bf16),
        ]
        + RowGather.scratch * 3
        + [DMA, DMA((16,)), DMA((16,)), DMA((8,)), DMA((8,)), DMA, DMA, DMA((8,)), DMA((8,))],
        compiler_params=pltpu.CompilerParams(
            collective_id=number, has_side_effects=True, vmem_limit_bytes=16 * 2**20
        ),
        name="entry_gather",
    )(x, query, key, value, small, out, routes)


def last_kernel(
    d_raw, weight, side, d_branch, d_logits, hidden_ref, att_ref, hid_ref, one_ref, a_out, w_out,
    hidden, att, hid, parts, w_parts, a_pack, landed, part, w_sum, w_landed, w_mine,
    in_sem, wlocal, wsend, wrecv, psend, precv, plocal, osend, orecv, olocal, xsend, xrecv, *scatters,
):
    place = my_place()
    core = place[4]
    dp, ctx = dp_of(place), ctx_of(place)
    barrier = greet(
        [device_at(dp, lax.rem(ctx + k, N_CTX)) for k in range(1, N_CTX)]
        + [device_at(lax.rem(dp + k, N_DP), ctx) for k in range(1, N_DP)]
    )
    loads = [
        pltpu.make_async_copy(att_ref.at[lax.div(ctx, 2), core], att, in_sem.at[0]),
        pltpu.make_async_copy(hid_ref, hid, in_sem.at[1]),
        pltpu.make_async_copy(hidden_ref, hidden, in_sem.at[2]),
    ]
    for load in loads:
        load.start()

    def back(c, _):
        here = pl.ds(pl.multiple_of(c * ROWS, ROWS), ROWS)
        parts[lax.div(c, 2), lax.rem(c, 2)] = dot_last(d_raw[here, :], weight[...]).astype(bf16)
        return 0

    lax.fori_loop(0, N_CTX, back, 0)
    pl.semaphore_wait(barrier, 22)
    rows = RowScatter(place, lambda chip, c: parts.at[chip, c], *scatters[:10])
    outs = RowScatter(place, lambda chip, c: w_parts.at[chip, c], *scatters[10:])
    for n in range(8):
        rows.start(n)
    for load in loads:
        load.wait()

    def heads(k, _):
        here = pl.ds(pl.multiple_of(k * ROWS, ROWS), ROWS)
        grad = dot_first(hidden[:, here], d_raw[...])
        gain = jnp.sum(grad * weight[here, :].astype(f32), axis=1, keepdims=True)
        lane = lax.broadcasted_iota(jnp.int32, (ROWS, 128), 1)
        extra = side[here, :]
        high = grad[:, 128:] + dot_first(hid[:, here], d_logits[...])
        high = jnp.where(lane == 64, gain * extra[:, 0:1], jnp.where(lane == 65, extra[:, 1:2], high))
        a_pack[k, :, :128] = grad[:, :128].astype(bf16)
        a_pack[k, :, 128:] = high.astype(bf16)
        return 0

    lax.fori_loop(0, N_DP, heads, 0)
    first, second, third = [], [], []
    for k in range(1, N_DP):
        to = lax.rem(dp + k, N_DP)
        first.append(remote(a_pack.at[to], landed.at[k], wsend.at[k], wrecv.at[k], device_at(to, ctx)))
        third.append(
            remote(
                w_sum.at[pl.ds(pl.multiple_of(to * 16, 16), 16)],
                w_landed.at[k],
                osend.at[k],
                orecv.at[k],
                device_at(to, ctx),
            )
        )
    for copy in first:
        copy.start()
    own = pltpu.make_async_copy(a_pack.at[dp], landed.at[0], wlocal)
    own.start()
    rows.step(0)
    rows.step(1)

    def products(k, _):
        here = pl.ds(pl.multiple_of(k * ROWS, ROWS), ROWS)
        total = dot_first(att[:, here], d_branch[...]).astype(bf16)
        to = pl.ds(pl.multiple_of(k * 16, 16), 16)
        for g in range(8):
            for c in range(2):
                w_parts[g, c, to, :] = total[g * 16 : (g + 1) * 16, c * 512 : (c + 1) * 512]
        return 0

    lax.fori_loop(0, N_DP, products, 0)
    for n in range(8):
        outs.start(n)
    for n in range(2, 6):
        rows.step(n)
    outs.step(0)
    outs.step(1)
    own.wait()
    for copy in first:
        copy.wait_recv()
    total = landed[0].astype(f32)
    for k in range(1, N_DP):
        total = total + landed[k].astype(f32)
    part[...] = total.reshape(part.shape)
    for k in range(1, N_CTX):
        to = lax.rem(ctx + k, N_CTX)
        second.append(remote(part.at[to], a_out.at[ctx], psend.at[k], precv.at[k], device_at(dp, to)))
    for copy in second:
        copy.start()
    mine = pltpu.make_async_copy(part.at[ctx], a_out.at[ctx], plocal)
    mine.start()
    rows.step(6)
    for n in range(2, 6):
        outs.step(n)
    one_ref[...] = rows.step(7)
    outs.step(6)
    w_sum[...] = outs.step(7)
    for copy in third:
        copy.start()
    own = pltpu.make_async_copy(w_sum.at[pl.ds(pl.multiple_of(dp * 16, 16), 16)], w_landed.at[0], olocal)
    own.start()
    own.wait()
    for copy in third:
        copy.wait_recv()
    total = w_landed[0]
    for k in range(1, N_DP):
        total = total + w_landed[k]
    w_mine[...] = total.reshape(2, 8, 512)
    swap = remote(w_mine.at[1 - core], w_out.at[core], xsend, xrecv, sibling_of(place))
    swap.start()
    keep = pltpu.make_async_copy(w_mine.at[core], w_out.at[core], in_sem.at[0])
    swap_in = remote(w_mine.at[1 - core], w_out.at[1 - core], xsend, xrecv, sibling_of(place))
    swap_in.wait_recv()
    swap.wait_send()
    keep.start()
    keep.wait()
    mine.wait()
    for copy in second:
        copy.wait_recv()
    rows.release()
    outs.release()
    rows.finish()
    outs.finish()
    for copy in first + second + third:
        copy.wait_send()


def last(d_raw, weight, side, d_branch, d_logits, hidden, att, hid, number):
    v = lambda *shape: pltpu.VMEM(shape, bf16)
    return pl.pallas_call(
        last_kernel,
        out_shape=(
            jax.ShapeDtypeStruct((ROWS, D), f32),
            jax.ShapeDtypeStruct((N_CTX, 8, 256), f32),
            jax.ShapeDtypeStruct((2, 8, 512), f32),
        ),
        in_specs=[VMEM] * 5 + [ANY] * 3,
        out_specs=(VMEM,) * 3,
        scratch_shapes=[
            v(SEQ, D),
            v(ROWS, D),
            v(ROWS, D),
            v(8, 2, ROWS, D),
            v(8, 2, ROWS, 512),
            v(N_DP, ROWS, 256),
            v(N_DP, ROWS, 256),
            pltpu.VMEM((N_CTX, 8, 256), f32),
            pltpu.VMEM((ROWS, 512), f32),
            pltpu.VMEM((N_DP, 16, 512), f32),
            pltpu.VMEM((2, 8, 512), f32),
            DMA((3,)),
            DMA,
            DMA((8,)),
            DMA((8,)),
            DMA((16,)),
            DMA((16,)),
            DMA,
            DMA((8,)),
            DMA((8,)),
            DMA,
            DMA,
            DMA,
        ]
        + RowScatter.scratch(ROWS, D)
        + RowScatter.scratch(ROWS, 512),
        compiler_params=pltpu.CompilerParams(
            collective_id=number, has_side_effects=True, vmem_limit_bytes=48 * 2**20
        ),
        name="last_sums",
    )(d_raw, weight, side, d_branch, d_logits, hidden, att, hid)


def experts_kernel(
    tok_ref, att_ref, wo_ref, m_ref, router_ref, gain_ref, cot_ref, w_ref,
    out_ref, res_ref, d_res_ref, d_branch_ref, d_logits_ref, hid_ref, gain_grad_ref, g_ref, heads_ref,
    pool, members, win, wide, picks, facts_all, gates_all, logits_all, gate_slot, dg_slot,
    rows, tops, result, hidden, d_mid, own_rows, d_heads,
    in_sem, tok_sem, hsend, hrecv, *scatters,
):
    body = pl.ds(0, D)
    loads = [
        pltpu.make_async_copy(wo_ref, wide, in_sem.at[0]),
        pltpu.make_async_copy(m_ref, members, in_sem.at[1]),
        pltpu.make_async_copy(w_ref, win, in_sem.at[2]),
    ]
    place = my_place()
    core = place[4]
    dp, ctx = dp_of(place), ctx_of(place)
    chip = lax.div(ctx, 2)

    def tokens_of(i):
        return result.at[i // 3, pl.ds(i % 3 * 256, 256)] if i < 6 else tops.at[0, pl.ds((i - 6) * 256, 256)]

    streams = []
    for i in range(8):
        streams.append(
            (
                pltpu.make_async_copy(tok_ref.at[i], tokens_of(i), tok_sem.at[0, i]),
                pltpu.make_async_copy(att_ref.at[i], pool.at[i, :, 0, :, body], tok_sem.at[1, i]),
            )
        )
    loads[0].start()
    for pair in streams[:2]:
        pair[0].start()
        pair[1].start()
    pl.semaphore_wait(greet([device_at(dp, lax.rem(ctx + k, N_CTX)) for k in range(1, N_CTX)]), 15)
    gather = RowGather(
        place,
        cot_ref,
        lambda p: pool.at[p[2] * 4 + p[3], p[4], 1, :, body],
        ROWS // 2,
        *scatters[20:],
    )
    gather.start()
    for pair in streams[2:]:
        pair[0].start()
        pair[1].start()
    for load in loads[1:]:
        load.start()
    line = lax.broadcasted_iota(jnp.int32, (8, EXTRA), 0)
    lane = lax.broadcasted_iota(jnp.int32, (8, EXTRA), 1)
    chosen = jnp.logical_and(line < 2, lane == 64 + 2 * ctx + line)
    chosen = jnp.where(chosen, 1.0, 0.0).astype(bf16)
    back = jnp.logical_and(line < 4, lane == jnp.where(line < 2, 0, 32) + 2 * ctx + lax.rem(line, 2))
    back = jnp.where(back, 1.0, 0.0).astype(bf16)
    before = lax.broadcasted_iota(jnp.int32, (ROWS, ROWS), 0) < lax.broadcasted_iota(
        jnp.int32, (ROWS, ROWS), 1
    )
    before = jnp.where(before, 1.0, 0.0).astype(bf16)
    slots = lax.broadcasted_iota(jnp.int32, (MOST, ROWS), 0).astype(f32)

    def second_norm(token, att):
        residual = token.astype(f32) + dot(att[:, :FF], wide[0]) + dot(att[:, FF:], wide[1])
        scale = lax.rsqrt(jnp.mean(residual * residual, axis=1, keepdims=True) + epsilon)
        normed = residual * scale
        return residual, scale, normed, (normed * gain_ref[...]).astype(bf16)

    def gates_of(logits, inside):
        logits = jnp.where(inside > 0.5, logits, -1e30)
        weights = jnp.exp(logits - jnp.max(logits, axis=1, keepdims=True))
        weights = jnp.where(inside > 0.5, weights, 0.0)
        return weights / jnp.sum(weights, axis=1, keepdims=True)

    loads[0].wait()
    for i in range(8):
        for copy in streams[i]:
            copy.wait()
        att = pool[i, :, 0, :, :D].reshape(2 * ROWS, D)
        token = (
            result[i // 3, i % 3 * 256 : i % 3 * 256 + 256]
            if i < 6
            else tops[0, (i - 6) * 256 : (i - 5) * 256]
        )
        hid = second_norm(token, att)[3]
        pool[i, :, 0, :, :D] = hid.reshape(2, ROWS, D)
        logits_all[i * 256 : (i + 1) * 256] = dot(hid, router_ref[...])
        if i == 2:
            gather.step(0)
    gather.step(1)
    gather.step(2)
    loads[1].wait()
    for half in range(2):
        inside = members[8 * half : 8 * half + 8].reshape(8 * ROWS, EXTRA)
        gates = gates_of(logits_all[1024 * half : 1024 * (half + 1)], inside.astype(f32))
        high = gates.astype(bf16)
        rest = (gates - high.astype(f32)).astype(bf16)
        facts = dot_last(chosen, inside)
        lines = dot_last(chosen, high) + dot_last(chosen, rest)
        for c in range(8):
            facts_all[8 * half + c] = facts[:, c * ROWS : (c + 1) * ROWS]
            gates_all[8 * half + c] = lines[:, c * ROWS : (c + 1) * ROWS]

    def pick(i, _):
        for k in range(4):
            c = i * 4 + k
            facts, lines = facts_all[c], gates_all[c]
            order = dot(facts.astype(bf16), before)
            here = pl.ds(pl.multiple_of(c * MOST, MOST), MOST)
            both = []
            for e in range(2):
                member = facts[e : e + 1]
                onehot = jnp.where(jnp.logical_and(order[e : e + 1] == slots, member > 0.5), 1.0, 0.0)
                gate_slot[e, here] = jnp.sum(onehot * lines[e : e + 1], axis=1, keepdims=True)
                both.append(onehot.astype(bf16))
            both = jnp.concatenate(both, axis=0)
            picks[c] = both
            taken = dot(both, pool[i * 2 + k // 2, k % 2, 0, :, :D]).astype(bf16)
            rows[0, here] = taken[:MOST]
            rows[1, here] = taken[MOST:]
        return 0

    lax.fori_loop(0, 4, pick, 0)
    for n in range(3, 5):
        gather.step(n)
    loads[2].wait()
    for e in range(2):
        for k in range(N_DP):
            for q in range(8):
                wide[e, q * 64 : (q + 1) * 64, k * ROWS : (k + 1) * ROWS] = win[
                    k, e, ROWS:, q * ROWS : (q + 1) * ROWS
                ]
    tile = 256

    def pick_tops(i, _):
        for k in range(4):
            c = i * 4 + k
            here = pl.ds(pl.multiple_of(c * MOST, MOST), MOST)
            taken = dot(picks[c], pool[i * 2 + k // 2, k % 2, 1, :, :D]).astype(bf16)
            tops[0, here] = taken[:MOST]
            tops[1, here] = taken[MOST:]
        return 0

    def forth(e, t):
        here = pl.ds(t * tile, tile)
        both = dot(rows[e, here], win[:, e, :ROWS].reshape(D, 2 * FF))
        gate_part, up_part = both[:, :FF], both[:, FF:]
        sigmoid = 1.0 / (1.0 + jnp.exp(-gate_part))
        silu = gate_part * sigmoid
        middle = (silu * up_part).astype(bf16)
        hidden[e, here] = middle
        d_mid[e, here, :FF] = (up_part * (sigmoid * (1.0 + gate_part * (1.0 - sigmoid)))).astype(bf16)
        d_mid[e, here, FF:] = silu.astype(bf16)
        result[e, here] = dot(middle, wide[e]).astype(bf16)

    def backward(e, t):
        here = pl.ds(t * tile, tile)
        top = tops[e, here].astype(f32)
        dg_slot[e, here] = jnp.sum(top * result[e, here].astype(f32), axis=1, keepdims=True)
        d_result = (top * gate_slot[e, here]).astype(bf16)
        tops[e, here] = d_result
        d_middle = dot_last(d_result, wide[e])
        d_mid[e, here, :FF] = (d_middle * d_mid[e, here, :FF].astype(f32)).astype(bf16)
        d_mid[e, here, FF:] = (d_middle * d_mid[e, here, FF:].astype(f32)).astype(bf16)
        weight = win[:, e, :ROWS].reshape(D, 2 * FF)
        result[e, here] = dot_last(d_mid[e, here], weight).astype(bf16)

    def combine_out(i, _):
        for k in range(4):
            c = i * 4 + k
            here = pl.ds(pl.multiple_of(c * MOST, MOST), MOST)
            found = [(result[e, here].astype(f32) * gate_slot[e, here]).astype(bf16) for e in range(2)]
            found = jnp.concatenate(found, axis=0)
            pool[i * 2 + k // 2, k % 2, 0, :, :D] = dot_first(picks[c], found).astype(bf16)
        return 0

    def combine_back(i, _):
        for k in range(4):
            c = i * 4 + k
            here = pl.ds(pl.multiple_of(c * MOST, MOST), MOST)
            both = picks[c]
            found = jnp.concatenate([result[0, here], result[1, here]], axis=0)
            pool[i * 2 + k // 2, k % 2, 1, :, :D] = dot_first(both, found).astype(bf16)
            lines = [
                jnp.sum(
                    both[e * MOST : (e + 1) * MOST].astype(f32) * dg_slot[e, here], axis=0, keepdims=True
                )
                for e in range(2)
            ]
            high = [v.astype(bf16).astype(f32) for v in lines]
            rest = [v - h for v, h in zip(lines, high)]
            lines = jnp.concatenate(high + rest + [jnp.zeros((4, ROWS), f32)], axis=0).astype(bf16)
            pool[i * 2 + k // 2, k % 2, 1, :, D:] = dot_first(lines, back).astype(bf16)
        return 0

    for e in range(2):
        for t in range(3):
            forth(e, t)
            if e == 0 and t < 2:
                gather.step(5 + 2 * t)
                gather.step(6 + 2 * t)
    lax.fori_loop(0, 4, combine_out, 0)
    first = RowScatter(place, lambda h, c: pool.at[h, c, 0, :, body], *scatters[:10])
    second = RowScatter(place, lambda h, c: pool.at[h, c, 1], *scatters[10:20])
    for n in range(8):
        first.start(n)
    gather.finish()
    first.step(0)
    first.step(1)
    lax.fori_loop(0, 4, pick_tops, 0)
    plan = [(), (), (2, 3), (4, 5), (), ()]
    for e in range(2):
        for t in range(3):
            backward(e, t)
            for n in plan[3 * e + t]:
                first.step(n)
    lax.fori_loop(0, 4, combine_back, 0)
    for n in range(8):
        second.start(n)
    first.step(6)
    second.step(0)
    second.step(1)
    reload = [
        pltpu.make_async_copy(wo_ref, wide, in_sem.at[0]),
        pltpu.make_async_copy(cot_ref, own_rows.at[0], in_sem.at[1]),
        pltpu.make_async_copy(tok_ref.at[chip, pl.ds(core * ROWS, ROWS)], own_rows.at[1], tok_sem.at[0, 0]),
        pltpu.make_async_copy(att_ref.at[chip, core], own_rows.at[2], tok_sem.at[0, 1]),
    ]

    def weights(e, k):
        here = pl.ds(k * 256, 256)
        total = dot_first(rows[e, :, here], d_mid[e]).astype(bf16)
        win[2 * k, e, :ROWS] = total[:ROWS]
        win[2 * k + 1, e, :ROWS] = total[ROWS:]
        total = dot_first(hidden[e], tops[e, :, here]).astype(bf16)
        for q in range(8):
            win[2 * k, e, ROWS:, q * ROWS : (q + 1) * ROWS] = total[q * 64 : (q + 1) * 64, :ROWS]
            win[2 * k + 1, e, ROWS:, q * ROWS : (q + 1) * ROWS] = total[q * 64 : (q + 1) * 64, ROWS:]

    for copy in reload:
        copy.start()
    plan = [(), (), (), (), (2, 3), (), (4, 5), ()]
    for e in range(2):
        for k in range(4):
            weights(e, k)
            for n in plan[4 * e + k]:
                second.step(n)
    save = pltpu.make_async_copy(win, g_ref, in_sem.at[2])
    save.start()
    for copy in reload:
        copy.wait()
    residual, scale, normed, hid = second_norm(own_rows[1], own_rows[2])
    res_ref[...] = residual
    hid_ref[...] = hid
    gates = gates_of(dot(hid, router_ref[...]), members[ctx].astype(f32))
    second.step(6)
    out_ref[...] = first.step(7)
    total = second.step(7)
    d_gates = pltpu.roll(total[:, D:], 64, 1) + pltpu.roll(total[:, D:], 32, 1)
    d_picked = gates * (d_gates - jnp.sum(gates * d_gates, axis=1, keepdims=True))
    d_logits = d_picked.astype(bf16)
    d_logits_ref[...] = pltpu.roll(d_picked, 2, 1).astype(bf16)
    d_hid = total[:, :D] + dot_last(d_logits, router_ref[...])
    gain_grad_ref[...] = jnp.sum(d_hid * normed, axis=0, keepdims=True)
    d_normed = d_hid * gain_ref[...]
    inner = jnp.mean(d_normed * normed, axis=1, keepdims=True)
    d_res = own_rows[0].astype(f32) + scale * (d_normed - normed * inner)
    d_res_ref[...] = d_res
    d_branch = d_res.astype(bf16)
    d_branch_ref[...] = d_branch
    for s in range(2):
        d_att = dot_last(d_branch, wide[s]).astype(bf16)
        for g in range(4):
            d_heads[4 * s + g] = d_att[:, g * 128 : (g + 1) * 128]
    copies = []
    for k in range(1, N_CTX):
        to = lax.rem(ctx + k, N_CTX)
        copies.append(
            remote(
                d_heads.at[lax.div(to, 2)], heads_ref.at[ctx], hsend.at[k], hrecv.at[k], device_at(dp, to)
            )
        )
    for copy in copies:
        copy.start()
    own = pltpu.make_async_copy(d_heads.at[lax.div(ctx, 2)], heads_ref.at[ctx], in_sem.at[0])
    own.start()
    save.wait()
    own.wait()
    for copy in copies:
        copy.wait_recv()
    for copy in copies:
        copy.wait_send()
    first.release()
    second.release()
    first.finish()
    second.finish()


def experts(tok, att, wo, members, router, gain, cot, weights, number):
    slots = N_CTX * MOST
    v = lambda *shape: pltpu.VMEM(shape, bf16)
    column = pltpu.VMEM((2, slots, 1), f32)
    blocks = (8, 2, ROWS, D)
    return pl.pallas_call(
        experts_kernel,
        out_shape=(
            jax.ShapeDtypeStruct((ROWS, D), f32),
            jax.ShapeDtypeStruct((ROWS, D), f32),
            jax.ShapeDtypeStruct((ROWS, D), f32),
            jax.ShapeDtypeStruct((ROWS, D), bf16),
            jax.ShapeDtypeStruct((ROWS, EXTRA), bf16),
            jax.ShapeDtypeStruct((ROWS, D), bf16),
            jax.ShapeDtypeStruct((1, D), f32),
            jax.ShapeDtypeStruct(weights.shape, bf16),
            jax.ShapeDtypeStruct((N_CTX, ROWS, 128), bf16),
        ),
        in_specs=[ANY] * 4 + [VMEM] * 2 + [ANY] * 2,
        out_specs=(VMEM,) * 7 + (ANY,) * 2,
        scratch_shapes=[
            v(8, 2, 2, ROWS, D + EXTRA),
            v(N_CTX, ROWS, EXTRA),
            v(*weights.shape),
            v(2, FF, D),
            v(N_CTX, 2 * MOST, ROWS),
            pltpu.VMEM((N_CTX, 8, ROWS), f32),
            pltpu.VMEM((N_CTX, 8, ROWS), f32),
            pltpu.VMEM((SEQ, EXTRA), f32),
            column,
            column,
            v(2, slots, D),
            v(2, slots, D),
            v(2, slots, D),
            v(2, slots, FF),
            v(2, slots, 2 * FF),
            v(3, ROWS, D),
            v(8, ROWS, 128),
            DMA((3,)),
            DMA((2, 8)),
            DMA((16,)),
            DMA((16,)),
        ]
        + RowScatter.scratch(ROWS, D)
        + RowScatter.scratch(ROWS, D + EXTRA)
        + RowGather.scratch,
        compiler_params=pltpu.CompilerParams(
            collective_id=number, has_side_effects=True, vmem_limit_bytes=61 * 2**20
        ),
        cost_estimate=pl.CostEstimate(flops=15 * 10**9, bytes_accessed=30 * 2**20, transcendentals=2**20),
        name="experts_both_ways",
    )(tok.reshape(8, 2 * ROWS, D), att.reshape(blocks), wo.reshape(2, FF, D), members, router, gain, cot, weights)


def swap_halves(u):
    lane = lax.broadcasted_iota(jnp.int32, u.shape, 1)
    return jnp.where(lax.rem(lane, 64) < 32, pltpu.roll(u, 96, 1), pltpu.roll(u, 32, 1))


def attend_kernel(
    src, order, raw_ref, cos_ref, sin_ref, o_ref, padded, q_ref, k_ref, v_ref, lse_ref, out_nat
):
    core = lax.axis_index("core")
    for b in range(SEQ // BLOCK):
        rows = pl.ds(pl.multiple_of(src[b] * BLOCK, BLOCK), BLOCK)
        here = pl.ds(b * BLOCK, BLOCK)
        qk = raw_ref[rows, 0:128]
        qk = qk * cos_ref[here, :] + swap_halves(qk) * sin_ref[here, :]
        q_ref[here, :] = (qk[:, 0:64]).astype(bf16)
        k_ref[here, :] = (qk[:, 64:128]).astype(bf16)
        v_ref[here, :] = raw_ref[rows, 128:192].astype(bf16)
    step = 256
    for i in range(SEQ // step):
        length = (i + 1) * step
        here = pl.ds(i * step, step)
        scores = dot_last(q_ref[here, :], k_ref[0:length, :]) * 0.125
        row = i * step + lax.broadcasted_iota(jnp.int32, (step, length), 0)
        column = lax.broadcasted_iota(jnp.int32, (step, length), 1)
        scores = jnp.where(column <= row, scores, -1e30)
        top = jnp.max(scores, axis=1, keepdims=True)
        weights = jnp.exp(scores - top)
        total = jnp.sum(weights, axis=1, keepdims=True)
        lse_ref[here, :] = top + jnp.log(total)
        probs = (weights * (1.0 / total)).astype(bf16)
        out_nat[here, :] = dot(probs, v_ref[0:length, :])
    for b in range(SEQ // BLOCK):
        rows = pl.ds(pl.multiple_of(order[b] * BLOCK, BLOCK), BLOCK)
        here = pl.ds(b * BLOCK, BLOCK)
        out = out_nat[rows, :].astype(bf16)
        o_ref[here, :] = out
        empty = jnp.zeros_like(out)
        padded[here, :] = jnp.where(
            core == 0, jnp.concatenate([out, empty], axis=1), jnp.concatenate([empty, out], axis=1)
        )


def attend(src, order, raw, cosine, sine):
    head = jax.ShapeDtypeStruct((SEQ, HEAD_DIM), bf16)
    return pl.pallas_call(
        attend_kernel,
        out_shape=(
            head,
            jax.ShapeDtypeStruct((SEQ, 128), bf16),
            head,
            head,
            head,
            jax.ShapeDtypeStruct((SEQ, 1), f32),
        ),
        in_specs=[SMEM, SMEM, VMEM, VMEM, VMEM],
        out_specs=(VMEM,) * 6,
        scratch_shapes=[pltpu.VMEM((SEQ, HEAD_DIM), f32)],
        compiler_params=pltpu.CompilerParams(vmem_limit_bytes=48 * 2**20),
        cost_estimate=pl.CostEstimate(flops=10**9, bytes_accessed=6 * 2**20, transcendentals=2**21),
        name="attention_forward",
    )(src, order, raw, cosine, sine)


def heads_kernel(padded, att_out, mine, other, merged, msem, xsend, xrecv, *sems):
    place = my_place()
    core = place[4]
    pl.semaphore_wait(greet(chip_neighbours(place)), 4)
    half = SEQ // 2
    swap = remote(
        padded.at[pl.ds(pl.multiple_of((1 - core) * half, half), half)], other, xsend, xrecv,
        sibling_of(place),
    )
    swap.start()
    own = pltpu.make_async_copy(padded.at[pl.ds(pl.multiple_of(core * half, half), half)], mine, msem)
    own.start()
    own.wait()
    swap.wait_recv()
    merged[...] = mine[...] + other[...]

    def view(p):
        chip = p[2] * 4 + p[3]
        return att_out.at[
            pl.ds(pl.multiple_of(p[4] * half, half), half), pl.ds(pl.multiple_of(chip * 128, 128), 128)
        ]

    heads = RowGather(place, merged, view, half // 2, *sems)
    heads.start()
    heads.pass_on()
    heads.finish()
    swap.wait_send()


def gather_heads(padded, number):
    return pl.pallas_call(
        heads_kernel,
        out_shape=jax.ShapeDtypeStruct((SEQ, D), bf16),
        in_specs=[ANY],
        out_specs=ANY,
        scratch_shapes=[pltpu.VMEM((SEQ // 2, 128), bf16)] * 3 + [DMA] * 3 + RowGather.scratch,
        compiler_params=pltpu.CompilerParams(collective_id=number, has_side_effects=True),
        name="gather_heads",
    )(padded)


def attend_back_kernel(
    src, order, q_ref, k_ref, v_ref, lse_ref, do_ref, cos_ref, sin_ref, out_ref, do_nat, acc, done
):
    core = lax.axis_index("core")
    for b in range(SEQ // BLOCK):
        rows = pl.ds(pl.multiple_of(src[b] * BLOCK, BLOCK), BLOCK)
        pair = do_ref[rows, :].astype(f32)
        do_nat[pl.ds(b * BLOCK, BLOCK), :] = jnp.where(core == 0, pair[:, :64], pair[:, 64:])
    acc[...] = jnp.zeros_like(acc)
    step = 256
    for i in range(SEQ // step):
        length = (i + 1) * step
        here = pl.ds(i * step, step)
        query, d_out = q_ref[here, :], do_nat[here, :].astype(bf16)
        keys = k_ref[0:length, :]
        scores = dot_last(query, keys) * 0.125
        row = i * step + lax.broadcasted_iota(jnp.int32, (step, length), 0)
        column = lax.broadcasted_iota(jnp.int32, (step, length), 1)
        probs = jnp.where(column <= row, jnp.exp(scores - lse_ref[here, :]), 0.0)
        d_probs = dot_last(d_out, v_ref[0:length, :])
        delta = jnp.sum(probs * d_probs, axis=1, keepdims=True)
        d_scores = (probs * (d_probs - delta)).astype(bf16)
        acc[here, 0:64] = dot(d_scores, keys) * 0.125
        acc[0:length, 64:128] += dot_first(d_scores, query) * 0.125
        acc[0:length, 128:192] += dot_first(probs.astype(bf16), d_out)
    for b in range(SEQ // BLOCK):
        here = pl.ds(b * BLOCK, BLOCK)
        qk = acc[here, 0:128]
        qk = qk * cos_ref[here, :] - swap_halves(qk) * sin_ref[here, :]
        done[here, 0:128] = qk
        done[here, 128:256] = acc[here, 128:256]
    for b in range(SEQ // BLOCK):
        rows = pl.ds(pl.multiple_of(order[b] * BLOCK, BLOCK), BLOCK)
        out_ref[pl.ds(b * BLOCK, BLOCK), :] = done[rows, :].astype(bf16)


def attend_back(src, order, q, k, v, lse, d_out, cosine, sine):
    return pl.pallas_call(
        attend_back_kernel,
        out_shape=jax.ShapeDtypeStruct((SEQ, 256), bf16),
        in_specs=[SMEM, SMEM] + [VMEM] * 7,
        out_specs=VMEM,
        scratch_shapes=[
            pltpu.VMEM((SEQ, HEAD_DIM), f32),
            pltpu.VMEM((SEQ, 256), f32),
            pltpu.VMEM((SEQ, 256), f32),
        ],
        compiler_params=pltpu.CompilerParams(vmem_limit_bytes=56 * 2**20),
        cost_estimate=pl.CostEstimate(flops=3 * 10**9, bytes_accessed=6 * 2**20, transcendentals=2**21),
        name="attention_backward",
    )(src, order, q, k, v, lse, d_out, cosine, sine)


def rotary_tables():
    inverse = 10000.0 ** (-np.arange(32, dtype=np.float64) * 2.0 / HEAD_DIM)
    angles = np.arange(SEQ, dtype=np.float64)[:, None] * inverse[None, :]
    cosine, sine = np.cos(angles), np.sin(angles)
    return (
        np.tile(cosine, (1, 4)).astype(np.float32),
        np.concatenate([-sine, sine, -sine, sine], axis=1).astype(np.float32),
    )


def normalize(inputs, gain_values):
    scale_rows = lax.rsqrt(jnp.mean(inputs * inputs, axis=-1, keepdims=True) + epsilon)
    normed = inputs * scale_rows
    return (scale_rows, normed, (normed * gain_values.astype(f32)).astype(bf16))


def norm_backward(grad_in, normed, scale_rows, gain_values):
    grad_normed = grad_in * gain_values.astype(f32)
    inner = jnp.mean(grad_normed * normed, axis=-1, keepdims=True)
    return (scale_rows * (grad_normed - normed * inner), jnp.sum(grad_in * normed, axis=0))


def halves(value):
    high = lax.reduce_precision(value, 8, 7)
    return high.astype(bf16), (value - high).astype(bf16)


def local(
    tokens,
    cotangent,
    block_order,
    routes,
    norm_one,
    w_query,
    w_key,
    w_value,
    w_out,
    norm_two,
    w_router,
    expert_in,
    expert_out,
):
    ctx = lax.axis_index(CTX)
    cosine, sine = (jnp.asarray(t) for t in rotary_tables())
    order = jnp.stack([block_order, 2 * N_CTX - 1 - block_order], axis=1).reshape(-1)
    spots = jnp.arange(2 * N_CTX, dtype=jnp.int32)
    src = jnp.sum(jnp.where(order[None, :] == spots[:, None], spots[None, :], 0), axis=1)

    small = jnp.concatenate(
        [w_router, norm_one[:, None], norm_two[:, None], jnp.zeros((8, 30), bf16)], axis=1
    )
    tokens_all, packed_all, out_all, members = entry(
        tokens, w_query, w_key, w_value, small, w_out, routes, 0
    )
    down_packed = expert_out.reshape(2, 8, 64, ROWS).swapaxes(1, 2).reshape(2, 64, D)
    expert_all = lax.all_gather(jnp.concatenate([expert_in, down_packed], axis=1), DP, axis=0)
    low = packed_all[:, :, 8:, :].reshape(D, 128)
    weight = jnp.concatenate(
        [packed_all[:, :, :8, :].reshape(D, 128), low[:, :64], jnp.zeros((D, 64), bf16)], axis=1
    )
    router_weight, gain_one, gain_two = low[:, 64:96], low[:, 96], low[:, 97]
    out_weight = out_all.reshape(D, D)
    head_weight = lax.dynamic_slice_in_dim(out_weight, ctx * HEAD_DIM, HEAD_DIM, axis=0)

    tokens_float = tokens.astype(f32)
    scale_one, normed_one, _ = normalize(tokens_float, gain_one)
    _, _, hidden_one = normalize(tokens_all.reshape(SEQ, D).astype(f32), gain_one)
    raw = dot(hidden_one, weight)
    attended, padded, query, key, value, lse = attend(src, order, raw, cosine, sine)
    attended_all = gather_heads(padded, 1)

    router_wide = jnp.pad(router_weight, ((0, 0), (64, 32)))
    (
        out_sum,
        residual,
        d_residual,
        d_branch,
        d_logits,
        hidden_two,
        grad_gain_two,
        grad_experts,
        d_heads,
    ) = experts(
        tokens_all,
        attended_all,
        out_weight,
        members,
        router_wide,
        gain_two.astype(f32)[None, :],
        cotangent,
        expert_all,
        3,
    )
    output = residual + out_sum
    grad_experts = lax.psum_scatter(grad_experts, DP, scatter_dimension=0).astype(f32)
    grad_in = grad_experts[:, :ROWS]
    grad_down = grad_experts[:, ROWS:].reshape(2, 64, 8, ROWS).swapaxes(1, 2).reshape(2, FF, ROWS)

    d_raw = attend_back(src, order, query, key, value, lse, d_heads.reshape(SEQ, 128), cosine, sine)
    side = jnp.stack([1.0 / gain_one.astype(f32), grad_gain_two[0]], axis=1)
    side = jnp.pad(side, ((0, 0), (0, 126)))
    blocks = (8, 2, ROWS, D)
    d_hidden_one, a, b = last(
        d_raw,
        weight,
        side,
        d_branch,
        d_logits,
        hidden_one,
        attended_all.reshape(blocks),
        hidden_two,
        5,
    )
    d_norm_one, _ = norm_backward(d_hidden_one, normed_one, scale_one, gain_one)
    input_grad = d_residual + d_norm_one

    side_by_side = lambda v: jnp.moveaxis(v, 0, 1).reshape(8, -1)
    pairs = a.reshape(KV_HEADS, 2, 8, 256).sum(axis=1)
    common = jnp.sum(a[:, :, 192:], axis=0)
    return (
        output,
        input_grad,
        common[:, 0],
        side_by_side(a[:, :, 0:64]),
        side_by_side(pairs[:, :, 64:128]),
        side_by_side(pairs[:, :, 128:192]),
        side_by_side(b),
        common[:, 1],
        common[:, 2:34],
        grad_in,
        grad_down,
    )


def solution(mesh):
    split = Mesh(mesh.devices.reshape(2, 4, 2, 4, 2), AXES)
    rows = P(AXES, None)
    line = P(AXES)
    return jax.shard_map(
        local,
        mesh=split,
        in_specs=(
            rows,
            rows,
            P(),
            rows,
            line,
            rows,
            rows,
            rows,
            rows,
            line,
            rows,
            P(CTX, DP, None),
            P(CTX, None, DP),
        ),
        out_specs=(
            rows,
            rows,
            line,
            rows,
            rows,
            rows,
            rows,
            line,
            rows,
            P(CTX, DP, None),
            P(CTX, None, DP),
        ),
        check_vma=False,
    )
```

profile of v0, /device:TPU:1, one launch (start us, length us, event | category | flops | bytes accessed | tf_op | source)
XLA Modules:
  0.0 320.6 jit_solution(7352212656490931193)
XLA Ops:
  7.2 1.1 copy.72
  8.5 2.0 pad_maximum_fusion
  10.6 0.8 copy.62.routes_ref
  11.3 0.7 copy.60
  12.1 0.7 copy.61
  13.0 0.7 subtract_bitcast_fusion
  13.6 0.7 pad_add_fusion
  14.5 0.8 maximum_maximum_fusion.1.small_ref
  15.3 0.9 copy-done.1
  16.2 0.7 copy-done.10
  16.9 0.7 copy-done.11
  17.7 0.7 copy-done.12
  18.3 0.7 copy-done.13
  19.0 56.2 %entry_gather.1 = (bf16[16,128,1024]{2,1,0:T(8,128)(2,1)S(1)}, bf16[8,16,16,128]{3,2,1,0:T(8,128)(2,1)S(1)}, bf16[8,8,16,1024]{3,2,1,0:T(8,128)(2,1)S(1)}, bf16[16,128,128]{2,1,0:T(8,128)(2,1)S(1)}) custom-call(bf16[128,1024]{1,0:T(8,128)(2,1)S(1)} %copy-done.1, bf16[8,1024]{1,0:T(8,128)(2,1)S(1)} %copy-done.10, bf16[8,512]{1,0:T(8,128)(2,1)S(1)} %copy-done.12, ...), custom_call_target="tpu_custom_call" | custom-call | tf_op jit(solution)/shard_map/entry_gather/pallas_call | solution.py:344
  75.2 1.4 copy-done.16
  76.6 0.8 copy-done.18
  77.8 0.9 multiply_reduce_fusion
  78.8 1.6 convert_reduce_fusion.1
  80.4 1.3 fusion.1.hidden_ref
  81.7 1.9 copy-done.22
  83.7 2.6 fusion.10.raw_ref
  86.3 9.5 %attention_forward.1 = (bf16[2048,64]{1,0:T(8,128)(2,1)}, bf16[2048,128]{1,0:T(8,128)(2,1)S(1)}, bf16[2048,64]{1,0:T(8,128)(2,1)S(1)}, bf16[2048,64]{1,0:T(8,128...) custom-call(s32[32]{0:T(128)S(1)} %select_reduce_fusion.src, s32[32]{0:T(128)S(1)} %eq.15.order, ...), custom_call_target="tpu_custom_call" | custom-call | flops 1000000000 | bytes 6291456 | tf_op jit(solution)/shard_map/attention_forward/pallas_call | solution.py:941
  95.7 0.8 copy-done.6
  96.5 1.0 copy-done.17
  97.5 0.8 copy-done.19
  98.3 0.8 copy-done.20
  99.1 0.8 copy-done.21
  100.0 28.1 %gather_heads.1 = bf16[2048,1024]{1,0:T(8,128)(2,1)} custom-call(bf16[2048,128]{1,0:T(8,128)(2,1)} %copy-done.6), custom_call_target="tpu_custom_call" | custom-call | tf_op jit(solution)/shard_map/gather_heads/pallas_call | solution.py:990
  128.1 0.8 pad.8.router_ref
  128.9 88.2 %experts_both_ways.1 = (f32[128,1024]{1,0:T(8,128)}, f32[128,1024]{1,0:T(8,128)}, f32[128,1024]{1,0:T(8,128)}, bf16[128,1024]{1,0:T(8,128)(2,1)}, bf16[128,128]{...) custom-call(bf16[8,256,1024]{2,1,0:T(8,128)(2,1)} %bitcast.54, ...), custom_call_target="tpu_custom_call" | custom-call | flops 15000000512 | bytes 31457280 | tf_op jit(solution)/shard_map/experts_both_ways/pallas_call | solution.py:848
  217.2 0.9 copy-done.2
  218.2 0.2 copy.65
  218.7 13.5 %attention_backward.1.d_raw = bf16[2048,256]{1,0:T(8,128)(2,1)} custom-call(s32[32]{0:T(128)} %copy-done.15, s32[32]{0:T(128)} %copy-done.14, bf16[2048,64]{1,0:T(8,128)(2,1)} %copy-done.19, bf16[2048,64]{1,0:T(8,128)(2,1)} %copy-done.20, bf16[2048,64]{1,0:T(8,128)(2,1)} %copy-done.21, f32[2048,1]{1,0:T(8,128)} %copy-done.17, bf16[2048,128]{1,0:T(8,128)(2,1)} %bitcast.74, ...), custom_call_target="tpu_custom_call" | custom-call | flops 3000000000 | bytes 6291456 | tf_op jit(solution)/shard_map/attention_backward/pallas_call | solution.py:1038
  232.2 1.2 copy-done.5
  233.4 59.2 %last_sums.1 = (f32[128,1024]{1,0:T(8,128)S(1)}, f32[16,8,256]{2,1,0:T(8,128)S(1)}, f32[2,8,512]{2,1,0:T(8,128)S(1)}) custom-call(bf16[2048,256]{1,0:T(8,128)(2,1)S(1)} %copy-done.5, bf16[1024,256]{1,0:T(8,128)(2,1)S(1)} %maximum_maximum_fusion.weight, f32[1024,128]{1,0:T(8,128)S(1)} %select_maximum_fusion.side, bf16[128,1024]{1,0:T(8,128)(2,1)S(1)} %copy-done.7, ...), custom_call_target="tpu_custom_call" | custom-call | tf_op jit(solution)/shard_map/last_sums/pallas_call | solution.py:505
  292.7 0.7 reshape.129
  293.4 0.7 reshape.130
  294.2 0.7 reshape.127
  294.9 0.7 slice.57
  295.6 0.9 add.37
  296.4 0.7 slice_reduce_fusion.1
  297.1 0.2 fusion.4
  297.3 1.0 fusion.7
  298.4 11.1 %reduce-scatter.2.cloned.1.call-done = bf16[1,2,192,1024]{3,2,1,0:T(8,128)(2,1)} async-done(((bf16[8,2,192,1024]{3,2,1,0:T(8,128)(2,1)}), bf16[1,2,192,1024]{3,2,1,0:T(8,128)(2,1)}) %reduce-scatter.2.cloned.1.call-update) | async-done | bytes 786448 | tf_op jit(solution)/shard_map/reduce_scatter | solution.py:1148
  309.5 1.3 bitcast_convert_fusion
  310.8 1.1 slice.66
  312.1 0.9 copy.69
  313.0 0.6 copy.74
  (71 shorter events, 1.9 us)
Async XLA Ops:
  7.2 121.7 %all-gather.3.cloned.1.call-start = ((), (), s32[]{:S(2)}) async-start(), calls=%async_computation.2 | async-start | bytes 7077888 | tf_op jit(solution)/shard_map/all_gather | solution.py:1109
  10.5 299.0 %reduce-scatter.2.cloned.1.call-start = ((), (), s32[]{:S(2)}) async-start(), calls=%async_computation.1 | async-start | bytes 7077888 | tf_op jit(solution)/shard_map/reduce_scatter | solution.py:1148
  14.5 71.8 %copy-start.14 = (s32[32]{0:T(128)}, s32[32]{0:T(128)S(1)}, u32[]{:S(2)}) copy-start(s32[32]{0:T(128)S(1)} %eq.15.order) | copy-start | bytes 388
  15.3 1.0 copy-start.1
  16.2 0.7 copy-start.10
  16.9 0.7 copy-start.11
  17.6 0.7 copy-start.12
  18.3 0.7 copy-start.13
  75.2 1.4 copy-start.16
  76.6 0.8 copy-start.18
  77.4 4.3 %copy-start = (bf16[16,128,1024]{2,1,0:T(8,128)(2,1)}, bf16[16,128,1024]{2,1,0:T(8,128)(2,1)S(1)}, u32[]{:S(2)}) copy-start(bf16[16,128,1024]{2,1,0:T(8,128)(2,1)S(1)} %get-tuple-element.32) | copy-start | bytes 12582916
  77.8 8.5 %copy-start.15 = (s32[32]{0:T(128)}, s32[32]{0:T(128)S(1)}, u32[]{:S(2)}) copy-start(s32[32]{0:T(128)S(1)} %select_reduce_fusion.src) | copy-start | bytes 388
  81.7 1.9 copy-start.22
  83.7 2.6 copy-start.3
  83.7 2.6 copy-start.4
  95.7 0.8 copy-start.6
  96.5 1.0 copy-start.17
  97.5 0.8 copy-start.19
  98.3 0.8 copy-start.20
  99.1 0.8 copy-start.21
  217.1 1.0 copy-start.2
  217.1 1.1 copy-start.27
  217.1 1.3 copy-start.23
  218.7 13.5 %copy-start.7 = (bf16[128,1024]{1,0:T(8,128)(2,1)S(1)}, bf16[128,1024]{1,0:T(8,128)(2,1)}, u32[]{:S(2)}) copy-start(bf16[128,1024]{1,0:T(8,128)(2,1)} %get-tuple-element.46.d_branch) | copy-start | bytes 786436
  218.7 13.5 %copy-start.8 = (bf16[128,1024]{1,0:T(8,128)(2,1)S(1)}, bf16[128,1024]{1,0:T(8,128)(2,1)}, u32[]{:S(2)}) copy-start(bf16[128,1024]{1,0:T(8,128)(2,1)} %get-tuple-element.48.hid_ref) | copy-start | bytes 786436
  218.7 13.5 %copy-start.9 = (bf16[128,128]{1,0:T(8,128)(2,1)S(1)}, bf16[128,128]{1,0:T(8,128)(2,1)}, u32[]{:S(2)}) copy-start(bf16[128,128]{1,0:T(8,128)(2,1)} %get-tuple-element.47.d_logits) | copy-start | bytes 98308
  232.2 1.3 copy-start.5
  233.4 62.1 %copy-start.25 = (f32[128,1024]{1,0:T(8,128)S(1)}, f32[128,1024]{1,0:T(8,128)}, u32[]{:S(2)}) copy-start(f32[128,1024]{1,0:T(8,128)} %get-tuple-element.38) | copy-start | bytes 1572868
  233.4 62.1 %copy-start.26 = (f32[128,1024]{1,0:T(8,128)S(1)}, f32[128,1024]{1,0:T(8,128)}, u32[]{:S(2)}) copy-start(f32[128,1024]{1,0:T(8,128)} %get-tuple-element.37) | copy-start | bytes 1572868
  233.4 63.9 %copy-start.24 = (f32[128,1024]{1,0:T(8,128)S(1)}, f32[128,1024]{1,0:T(8,128)}, u32[]{:S(2)}) copy-start(f32[128,1024]{1,0:T(8,128)} %get-tuple-element.39) | copy-start | bytes 1572868
Sparse Core Ops, SparseCore 0:
  10.6 92.9 all-gather.2
  217.3 92.1 reduce-scatter.1
where the time goes:
time: 325 us; the launch traced here: 321 us
  Pallas kernels  255 us (78%)
  local copies, waits for them, and re-layouts  25.7 us (8%)
  between operations  14.6 us (4%)
  other arithmetic  12 us (4%)
  waiting for transfers between devices  11.2 us (3%)
    pallas_call x1, Pallas kernels, experts(): pl.pallas_call(experts_kernel, out_shape=(jax.ShapeDtypeStruct((ROWS, D),...  88.2 us
    pallas_call x1, Pallas kernels, last(): pl.pallas_call(last_kernel, out_shape=(jax.ShapeDtypeStruct((ROWS, D), f3...  59.2 us
    pallas_call x1, Pallas kernels, entry(): pl.pallas_call(entry_kernel, out_shape=(jax.ShapeDtypeStruct((N_CTX,) + x...  56.2 us
    pallas_call x1, Pallas kernels, gather_heads(): pl.pallas_call(heads_kernel, out_shape=jax.ShapeDtypeStruct((SEQ, D), bf1...  28.1 us
    unnamed x59, local copies, waits for them, and re-layouts  15.8 us
    pallas_call x1, Pallas kernels, attend_back(): pl.pallas_call(attend_back_kernel, out_shape=jax.ShapeDtypeStruct((SEQ, 2...  13.5 us
    reduce_scatter x1, waiting for transfers between devices, local(): lax.psum_scatter(grad_experts, DP, scatter_dimension=0).astype(f32)  11.1 us
    pallas_call x1, Pallas kernels, attend(): pl.pallas_call(attend_kernel, out_shape=(head, jax.ShapeDtypeStruct((SEQ,...  9.45 us
  transfers between devices with their start and end apart: 2, of which 1 were waited for; matrix products, arithmetic and copies ran while one was open for 6% of the time, Pallas kernels for 52%

commit v1 on v0

--- a/solution.py
+++ b/solution.py
@@ -148,6 +148,43 @@
         for n in range(10):
             self.back[n].wait_recv()
         for copy in self.out + self.passed:
+            copy.wait_send()
+
+
+def around(place, dz):
+    ylo, z, yhi, x, core = place
+    return (ylo, lax.rem(z + dz, 4), yhi, x, core)
+
+
+class PlaneRing:
+    scratch = [DMA, DMA((4,)), DMA((4,))]
+
+    def __init__(self, place, block, out, local, send, recv):
+        z, up, down = place[1], around(place, 1), around(place, 3)
+        below = out.at[down[1], pl.ds(0, 1)]
+        above = out.at[up[1], pl.ds(1, 1)]
+        self.own = pltpu.make_async_copy(block, out.at[z], local)
+        self.out = [
+            remote(block, out.at[z], send.at[0], recv.at[0], up),
+            remote(block, out.at[z], send.at[1], recv.at[1], down),
+            remote(below, below, send.at[2], recv.at[2], up),
+            remote(above, above, send.at[3], recv.at[3], down),
+        ]
+
+    def start(self):
+        self.out[0].start()
+        self.out[1].start()
+        self.own.start()
+
+    def step(self, n):
+        self.out[n].wait_recv()
+        self.out[2 + n].start()
+
+    def finish(self):
+        self.own.wait()
+        self.out[2].wait_recv()
+        self.out[3].wait_recv()
+        for copy in self.out:
             copy.wait_send()
 
 
@@ -251,11 +288,12 @@
 
 
 def entry_kernel(
-    x_ref, q_ref, k_ref, v_ref, small_ref, o_ref, routes_ref, x_out, w_out, o_out, m_out,
+    x_ref, q_ref, k_ref, v_ref, small_ref, o_ref, routes_ref, ein_ref, eout_ref,
+    x_out, w_out, o_out, m_out, ein_own, eout_own, ein_y, eout_y,
     w_pack, o_pad, o_other, o_mid, m_pack, *sems,
 ):
     row_sems, o_sems, m_sems, rest = sems[:5], sems[5:10], sems[10:15], sems[15:]
-    wlocal, wsend, wrecv, psend, precv, xsend, xrecv, osend, orecv = rest
+    wlocal, wsend, wrecv, psend, precv, xsend, xrecv, osend, orecv, ysend, yrecv = rest[:11]
     place = my_place()
     core = place[4]
     dp, ctx = dp_of(place), ctx_of(place)
@@ -266,6 +304,17 @@
     pl.semaphore_wait(barrier, 22)
     rows = RowGather(place, x_ref, lambda p: x_out.at[ctx_of(p)], x_ref.shape[0] // 2, *row_sems)
     rows.start()
+    rings = [
+        PlaneRing(place, ein_ref, ein_own, *rest[11:14]),
+        PlaneRing(place, eout_ref, eout_own, *rest[14:17]),
+    ]
+    for ring in rings:
+        ring.start()
+    beyond = (1 - place[0],) + place[1:]
+    across = [
+        remote(ein_ref, ein_y, ysend.at[0], yrecv.at[0], beyond),
+        remote(eout_ref, eout_y, ysend.at[1], yrecv.at[1], beyond),
+    ]
 
     out = o_ref[...].astype(f32)
     empty = jnp.zeros_like(out)
@@ -320,12 +369,18 @@
 
     outs = RowGather(place, o_mid, o_view, 4, *o_sems)
     outs.start()
-    for n in range(5):
+    rows.step(0)
+    for copy in across:
+        copy.start()
+    for n in range(1, 5):
         rows.step(n)
     for n in range(9):
         members.step(n)
     for n in range(3):
         outs.step(n)
+    for n in range(2):
+        for ring in rings:
+            ring.step(n)
     for n in range(5, 9):
         rows.step(n)
     for n in range(3, 9):
@@ -333,6 +388,10 @@
     rows.finish()
     members.finish()
     outs.finish()
+    for ring in rings:
+        ring.finish()
+    for copy in across:
+        copy.wait()
     for copy in second:
         copy.wait_recv()
     swap.wait_send()
@@ -340,7 +399,7 @@
         copy.wait_send()
 
 
-def entry(x, query, key, value, small, out, routes, number):
+def entry(x, query, key, value, small, out, routes, ein, eout, number):
     return pl.pallas_call(
         entry_kernel,
         out_shape=(
@@ -348,9 +407,13 @@
             jax.ShapeDtypeStruct((N_DP, N_CTX, 16, 128), bf16),
             jax.ShapeDtypeStruct((N_DP, 8, 16, D), bf16),
             jax.ShapeDtypeStruct((N_CTX, ROWS, EXTRA), bf16),
+            jax.ShapeDtypeStruct((4,) + ein.shape, bf16),
+            jax.ShapeDtypeStruct((4,) + eout.shape, bf16),
+            jax.ShapeDtypeStruct(ein.shape, bf16),
+            jax.ShapeDtypeStruct(eout.shape, bf16),
         ),
-        in_specs=[ANY] + [VMEM] * 6,
-        out_specs=(ANY,) * 4,
+        in_specs=[ANY] + [VMEM] * 6 + [ANY] * 2,
+        out_specs=(ANY,) * 8,
         scratch_shapes=[
             pltpu.VMEM((N_CTX, 16, 128), bf16),
             pltpu.VMEM((2, 16, 512), bf16),
@@ -359,12 +422,14 @@
             pltpu.VMEM((ROWS, EXTRA), bf16),
         ]
         + RowGather.scratch * 3
-        + [DMA, DMA((16,)), DMA((16,)), DMA((8,)), DMA((8,)), DMA, DMA, DMA((8,)), DMA((8,))],
+        + [DMA, DMA((16,)), DMA((16,)), DMA((8,)), DMA((8,)), DMA, DMA, DMA((8,)), DMA((8,))]
+        + [DMA((2,)), DMA((2,))]
+        + PlaneRing.scratch * 2,
         compiler_params=pltpu.CompilerParams(
             collective_id=number, has_side_effects=True, vmem_limit_bytes=16 * 2**20
         ),
         name="entry_gather",
-    )(x, query, key, value, small, out, routes)
+    )(x, query, key, value, small, out, routes, ein, eout)
 
 
 def last_kernel(
@@ -546,9 +611,9 @@
 
 
 def experts_kernel(
-    tok_ref, att_ref, wo_ref, m_ref, router_ref, gain_ref, cot_ref, w_ref,
+    tok_ref, att_ref, wo_ref, m_ref, router_ref, gain_ref, cot_ref, ein_own, ein_far, eout_own, eout_far,
     out_ref, res_ref, d_res_ref, d_branch_ref, d_logits_ref, hid_ref, gain_grad_ref, g_ref, heads_ref,
-    pool, members, win, wide, picks, facts_all, gates_all, logits_all, gate_slot, dg_slot,
+    pool, members, win, down, wide, picks, facts_all, gates_all, logits_all, gate_slot, dg_slot,
     rows, tops, result, hidden, d_mid, own_rows, d_heads,
     in_sem, tok_sem, hsend, hrecv, *scatters,
 ):
@@ -556,10 +621,16 @@
     loads = [
         pltpu.make_async_copy(wo_ref, wide, in_sem.at[0]),
         pltpu.make_async_copy(m_ref, members, in_sem.at[1]),
-        pltpu.make_async_copy(w_ref, win, in_sem.at[2]),
     ]
     place = my_place()
     core = place[4]
+    near, far = pl.ds(place[0] * 4, 4), pl.ds(4 - place[0] * 4, 4)
+    loads += [
+        pltpu.make_async_copy(ein_own, win.at[near, :, pl.ds(0, ROWS)], in_sem.at[2]),
+        pltpu.make_async_copy(ein_far, win.at[far, :, pl.ds(0, ROWS)], in_sem.at[3]),
+        pltpu.make_async_copy(eout_own, down.at[near], in_sem.at[4]),
+        pltpu.make_async_copy(eout_far, down.at[far], in_sem.at[5]),
+    ]
     dp, ctx = dp_of(place), ctx_of(place)
     chip = lax.div(ctx, 2)
 
@@ -667,13 +738,11 @@
     lax.fori_loop(0, 4, pick, 0)
     for n in range(3, 5):
         gather.step(n)
-    loads[2].wait()
+    for load in loads[2:]:
+        load.wait()
     for e in range(2):
         for k in range(N_DP):
-            for q in range(8):
-                wide[e, q * 64 : (q + 1) * 64, k * ROWS : (k + 1) * ROWS] = win[
-                    k, e, ROWS:, q * ROWS : (q + 1) * ROWS
-                ]
+            wide[e, :, k * ROWS : (k + 1) * ROWS] = down[k, e]
     tile = 256
 
     def pick_tops(i, _):
@@ -841,6 +910,7 @@
 
 
 def experts(tok, att, wo, members, router, gain, cot, weights, number):
+    shape = (N_DP, 2, ROWS + 64, D)
     slots = N_CTX * MOST
     v = lambda *shape: pltpu.VMEM(shape, bf16)
     column = pltpu.VMEM((2, slots, 1), f32)
@@ -855,15 +925,16 @@
             jax.ShapeDtypeStruct((ROWS, EXTRA), bf16),
             jax.ShapeDtypeStruct((ROWS, D), bf16),
             jax.ShapeDtypeStruct((1, D), f32),
-            jax.ShapeDtypeStruct(weights.shape, bf16),
+            jax.ShapeDtypeStruct(shape, bf16),
             jax.ShapeDtypeStruct((N_CTX, ROWS, 128), bf16),
         ),
-        in_specs=[ANY] * 4 + [VMEM] * 2 + [ANY] * 2,
+        in_specs=[ANY] * 4 + [VMEM] * 2 + [ANY] * 5,
         out_specs=(VMEM,) * 7 + (ANY,) * 2,
         scratch_shapes=[
             v(8, 2, 2, ROWS, D + EXTRA),
             v(N_CTX, ROWS, EXTRA),
-            v(*weights.shape),
+            v(*shape),
+            v(N_DP, 2, FF, ROWS),
             v(2, FF, D),
             v(N_CTX, 2 * MOST, ROWS),
             pltpu.VMEM((N_CTX, 8, ROWS), f32),
@@ -878,7 +949,7 @@
             v(2, slots, 2 * FF),
             v(3, ROWS, D),
             v(8, ROWS, 128),
-            DMA((3,)),
+            DMA((6,)),
             DMA((2, 8)),
             DMA((16,)),
             DMA((16,)),
@@ -891,7 +962,7 @@
         ),
         cost_estimate=pl.CostEstimate(flops=15 * 10**9, bytes_accessed=30 * 2**20, transcendentals=2**20),
         name="experts_both_ways",
-    )(tok.reshape(8, 2 * ROWS, D), att.reshape(blocks), wo.reshape(2, FF, D), members, router, gain, cot, weights)
+    )(tok.reshape(8, 2 * ROWS, D), att.reshape(blocks), wo.reshape(2, FF, D), members, router, gain, cot, *weights)
 
 
 def swap_halves(u):
@@ -957,10 +1028,12 @@
     )(src, order, raw, cosine, sine)
 
 
-def heads_kernel(padded, att_out, mine, other, merged, msem, xsend, xrecv, *sems):
+def heads_kernel(
+    padded, ein_ref, eout_ref, att_out, ein_out, eout_out, mine, other, merged, msem, xsend, xrecv, *sems
+):
     place = my_place()
     core = place[4]
-    pl.semaphore_wait(greet(chip_neighbours(place)), 4)
+    pl.semaphore_wait(greet(chip_neighbours(place) + [around(place, 1), around(place, 3)]), 6)
     half = SEQ // 2
     swap = remote(
         padded.at[pl.ds(pl.multiple_of((1 - core) * half, half), half)], other, xsend, xrecv,
@@ -979,23 +1052,44 @@
             pl.ds(pl.multiple_of(p[4] * half, half), half), pl.ds(pl.multiple_of(chip * 128, 128), 128)
         ]
 
-    heads = RowGather(place, merged, view, half // 2, *sems)
+    heads = RowGather(place, merged, view, half // 2, *sems[:5])
     heads.start()
-    heads.pass_on()
+    rings = [
+        PlaneRing(place, ein_ref, ein_out, *sems[5:8]),
+        PlaneRing(place, eout_ref, eout_out, *sems[8:11]),
+    ]
+    for ring in rings:
+        ring.start()
+    for n in range(5):
+        heads.step(n)
+    for n in range(2):
+        for ring in rings:
+            ring.step(n)
+    for n in range(5, 9):
+        heads.step(n)
     heads.finish()
+    for ring in rings:
+        ring.finish()
     swap.wait_send()
 
 
-def gather_heads(padded, number):
+def gather_heads(padded, ein, eout, number):
     return pl.pallas_call(
         heads_kernel,
-        out_shape=jax.ShapeDtypeStruct((SEQ, D), bf16),
-        in_specs=[ANY],
-        out_specs=ANY,
-        scratch_shapes=[pltpu.VMEM((SEQ // 2, 128), bf16)] * 3 + [DMA] * 3 + RowGather.scratch,
+        out_shape=(
+            jax.ShapeDtypeStruct((SEQ, D), bf16),
+            jax.ShapeDtypeStruct((4,) + ein.shape, bf16),
+            jax.ShapeDtypeStruct((4,) + eout.shape, bf16),
+        ),
+        in_specs=[ANY] * 3,
+        out_specs=(ANY,) * 3,
+        scratch_shapes=[pltpu.VMEM((SEQ // 2, 128), bf16)] * 3
+        + [DMA] * 3
+        + RowGather.scratch
+        + PlaneRing.scratch * 2,
         compiler_params=pltpu.CompilerParams(collective_id=number, has_side_effects=True),
         name="gather_heads",
-    )(padded)
+    )(padded, ein, eout)
 
 
 def attend_back_kernel(
@@ -1102,11 +1196,9 @@
     small = jnp.concatenate(
         [w_router, norm_one[:, None], norm_two[:, None], jnp.zeros((8, 30), bf16)], axis=1
     )
-    tokens_all, packed_all, out_all, members = entry(
-        tokens, w_query, w_key, w_value, small, w_out, routes, 0
-    )
-    down_packed = expert_out.reshape(2, 8, 64, ROWS).swapaxes(1, 2).reshape(2, 64, D)
-    expert_all = lax.all_gather(jnp.concatenate([expert_in, down_packed], axis=1), DP, axis=0)
+    tokens_all, packed_all, out_all, members, in_own, down_own, in_beyond, down_beyond = entry(
+        tokens, w_query, w_key, w_value, small, w_out, routes, expert_in, expert_out, 0
+    )
     low = packed_all[:, :, 8:, :].reshape(D, 128)
     weight = jnp.concatenate(
         [packed_all[:, :, :8, :].reshape(D, 128), low[:, :64], jnp.zeros((D, 64), bf16)], axis=1
@@ -1120,7 +1212,7 @@
     _, _, hidden_one = normalize(tokens_all.reshape(SEQ, D).astype(f32), gain_one)
     raw = dot(hidden_one, weight)
     attended, padded, query, key, value, lse = attend(src, order, raw, cosine, sine)
-    attended_all = gather_heads(padded, 1)
+    attended_all, in_far, down_far = gather_heads(padded, in_beyond, down_beyond, 1)
 
     router_wide = jnp.pad(router_weight, ((0, 0), (64, 32)))
     (
@@ -1141,7 +1233,7 @@
         router_wide,
         gain_two.astype(f32)[None, :],
         cotangent,
-        expert_all,
+        (in_own, in_far, down_own, down_far),
         3,
     )
     output = residual + out_sum

time: 325 us -> 341 us (1.049)
  Pallas kernels: 255 us -> 268 us
  local copies, waits for them, and re-layouts: 25.7 us -> 29.7 us
    pallas_call x1, Pallas kernels: 56.2 us -> 63.9 us  [entry(): pl.pallas_call(entry_kernel, out_shape=(jax.ShapeDtypeStruct((N_CTX,) + x...]
    pallas_call x1, Pallas kernels: 28.1 us -> 32.7 us  [gather_heads(): pl.pallas_call(heads_kernel, out_shape=(jax.ShapeDtypeStruct((SEQ, D), bf...]
    unnamed x59 -> x75, local copies, waits for them, and re-layouts: 15.8 us -> 20 us
  transfers between devices with their start and end apart: 2 -> 1, of which waited for: 1 -> 1; matrix products, arithmetic and copies ran while one was open for 6% -> 2% of each run, Pallas kernels for 52% -> 22%
where the time goes in v1:
time: 341 us; the launch traced here: 336 us
  Pallas kernels  268 us (79%)
  local copies, waits for them, and re-layouts  29.7 us (9%)
  between operations  14.6 us (4%)
  other arithmetic  10.8 us (3%)
  waiting for transfers between devices  10.3 us (3%)
    pallas_call x1, Pallas kernels, experts(): pl.pallas_call(experts_kernel, out_shape=(jax.ShapeDtypeStruct((ROWS, D),...  89.3 us
    pallas_call x1, Pallas kernels, entry(): pl.pallas_call(entry_kernel, out_shape=(jax.ShapeDtypeStruct((N_CTX,) + x...  63.9 us
    pallas_call x1, Pallas kernels, last(): pl.pallas_call(last_kernel, out_shape=(jax.ShapeDtypeStruct((ROWS, D), f3...  59.5 us
    pallas_call x1, Pallas kernels, gather_heads(): pl.pallas_call(heads_kernel, out_shape=(jax.ShapeDtypeStruct((SEQ, D), bf...  32.7 us
    unnamed x75, local copies, waits for them, and re-layouts  20 us
    pallas_call x1, Pallas kernels, attend_back(): pl.pallas_call(attend_back_kernel, out_shape=jax.ShapeDtypeStruct((SEQ, 2...  13.4 us
    reduce_scatter x1, waiting for transfers between devices, local(): lax.psum_scatter(grad_experts, DP, scatter_dimension=0).astype(f32)  10.3 us
    pallas_call x1, Pallas kernels, attend(): pl.pallas_call(attend_kernel, out_shape=(head, jax.ShapeDtypeStruct((SEQ,...  9.53 us
  transfers between devices with their start and end apart: 1, of which 1 were waited for; matrix products, arithmetic and copies ran while one was open for 2% of the time, Pallas kernels for 22%

profile of v1, /device:TPU:1, one launch (start us, length us, event | category | flops | bytes accessed | tf_op | source)
XLA Modules:
  0.0 336.4 jit_solution(16134131051145296664)
XLA Ops:
  7.2 0.8 copy.58.routes_ref
  8.0 0.7 copy.56
  8.8 0.7 copy.57
  9.6 0.8 maximum_maximum_fusion.1.small_ref
  10.3 0.9 copy-done.1
  11.3 1.0 copy-done.6
  12.3 0.9 copy-done.12
  13.3 0.7 copy-done.14
  14.0 0.7 copy-done.15
  14.7 0.7 copy-done.16
  15.4 0.7 copy-done.17
  16.1 63.9 %entry_gather.1 = (bf16[16,128,1024]{2,1,0:T(8,128)(2,1)S(1)}, bf16[8,16,16,128]{3,2,1,0:T(8,128)(2,1)S(1)}, bf16[8,8,16,1024]{3,2,1,0:T(8,128)(2,1)S(1)}, bf16[...) custom-call(bf16[128,1024]{1,0:T(8,128)(2,1)S(1)} %copy-done.1, ...), custom_call_target="tpu_custom_call" | custom-call | tf_op jit(solution)/shard_map/entry_gather/pallas_call | solution.py:403
  80.0 0.8 copy-done.7
  80.8 1.3 copy-done.20
  82.1 1.4 copy-done.21
  83.5 1.0 copy-done.22
  84.5 1.0 fusion.9
  85.5 2.1 convert_reduce_fusion.1
  87.7 0.9 multiply_reduce_fusion
  89.0 0.9 pad.8.router_ref
  89.9 3.0 fusion.1.hidden_ref
  93.1 2.0 copy-done.28
  95.0 2.6 fusion.10.raw_ref
  97.7 9.5 %attention_forward.1 = (bf16[2048,64]{1,0:T(8,128)(2,1)}, bf16[2048,128]{1,0:T(8,128)(2,1)S(1)}, bf16[2048,64]{1,0:T(8,128)(2,1)S(1)}, bf16[2048,64]{1,0:T(8,128...) custom-call(s32[32]{0:T(128)S(1)} %select_reduce_fusion.src, s32[32]{0:T(128)S(1)} %eq.15.order, ...), custom_call_target="tpu_custom_call" | custom-call | flops 1000000000 | bytes 6291456 | tf_op jit(solution)/shard_map/attention_forward/pallas_call | solution.py:1012
  107.2 0.8 copy-done.8
  108.0 1.1 copy-done.23
  109.1 0.8 copy-done.25
  109.8 0.8 copy-done.26
  110.7 0.8 copy-done.27
  111.5 32.7 %gather_heads.1 = (bf16[2048,1024]{1,0:T(8,128)(2,1)}, bf16[4,2,128,1024]{3,2,1,0:T(8,128)(2,1)}, bf16[4,2,512,128]{3,2,1,0:T(8,128)(2,1)}) custom-call(bf16[2048,128]{1,0:T(8,128)(2,1)} %copy-done.8, bf16[2,128,1024]{2,1,0:T(8,128)(2,1)} %copy-done.7, bf16[2,512,128]{2,1,0:T(8,128)(2,1)} %copy-done.9), custom_call_target="tpu_custom_call" | custom-call | tf_op jit(solution)/shard_map/gather_heads/pallas_call | solution.py:1077
  144.2 89.3 %experts_both_ways.1 = (f32[128,1024]{1,0:T(8,128)}, f32[128,1024]{1,0:T(8,128)}, f32[128,1024]{1,0:T(8,128)}, bf16[128,1024]{1,0:T(8,128)(2,1)}, bf16[128,128]{...) custom-call(bf16[8,256,1024]{2,1,0:T(8,128)(2,1)} %bitcast.47, ...), custom_call_target="tpu_custom_call" | custom-call | flops 15000000512 | bytes 31457280 | tf_op jit(solution)/shard_map/experts_both_ways/pallas_call | solution.py:918
  233.6 0.6 copy-done.34
  234.8 13.4 %attention_backward.1.d_raw = bf16[2048,256]{1,0:T(8,128)(2,1)} custom-call(s32[32]{0:T(128)} %copy-done.19, s32[32]{0:T(128)} %copy-done.18, bf16[2048,64]{1,0:T(8,128)(2,1)} %copy-done.25, bf16[2048,64]{1,0:T(8,128)(2,1)} %copy-done.26, bf16[2048,64]{1,0:T(8,128)(2,1)} %copy-done.27, f32[2048,1]{1,0:T(8,128)} %copy-done.23, bf16[2048,128]{1,0:T(8,128)(2,1)} %bitcast.64, ...), custom_call_target="tpu_custom_call" | custom-call | flops 3000000000 | bytes 6291456 | tf_op jit(solution)/shard_map/attention_backward/pallas_call | solution.py:1132
  248.3 1.2 copy-done.5
  249.5 59.5 %last_sums.1 = (f32[128,1024]{1,0:T(8,128)S(1)}, f32[16,8,256]{2,1,0:T(8,128)S(1)}, f32[2,8,512]{2,1,0:T(8,128)S(1)}) custom-call(bf16[2048,256]{1,0:T(8,128)(2,1)S(1)} %copy-done.5, bf16[1024,256]{1,0:T(8,128)(2,1)S(1)} %maximum_maximum_fusion.weight, f32[1024,128]{1,0:T(8,128)S(1)} %select_maximum_fusion.side, bf16[128,1024]{1,0:T(8,128)(2,1)S(1)} %copy-done.10, ...), custom_call_target="tpu_custom_call" | custom-call | tf_op jit(solution)/shard_map/last_sums/pallas_call | solution.py:570
  309.2 0.7 reshape.121
  309.9 0.7 reshape.122
  310.6 0.7 reshape.119
  311.3 0.7 slice.57
  312.0 0.9 add.37
  312.9 0.7 slice_reduce_fusion.1
  313.7 0.2 fusion.4
  314.0 1.0 fusion.7
  315.0 10.3 %reduce-scatter.2.cloned.1.call-done = bf16[1,2,192,1024]{3,2,1,0:T(8,128)(2,1)} async-done(((bf16[8,2,192,1024]{3,2,1,0:T(8,128)(2,1)}), bf16[1,2,192,1024]{3,2,1,0:T(8,128)(2,1)}) %reduce-scatter.2.cloned.1.call-update) | async-done | bytes 786448 | tf_op jit(solution)/shard_map/reduce_scatter | solution.py:1240
  325.2 1.3 bitcast_convert_fusion
  326.6 1.1 slice.66
  327.8 0.9 copy.64
  328.7 0.6 copy.67
  (81 shorter events, 2.0 us)
Async XLA Ops:
  7.2 81.5 %copy-start.35 = (s32[16]{0:T(128)S(1)}, s32[16]{0:T(128)}, u32[]{:S(2)}) copy-start(s32[16]{0:T(128)} %param.17) | copy-start | bytes 196
  7.2 318.1 %reduce-scatter.2.cloned.1.call-start = ((), (), s32[]{:S(2)}) async-start(), calls=%async_computation.1 | async-start | bytes 7077888 | tf_op jit(solution)/shard_map/reduce_scatter | solution.py:1240
  10.3 1.0 copy-start.1
  11.3 1.0 copy-start.6
  12.3 0.9 copy-start.12
  13.3 0.7 copy-start.14
  14.0 0.7 copy-start.15
  14.7 0.7 copy-start.16
  15.4 0.7 copy-start.17
  80.0 0.8 copy-start.7
  80.8 1.3 copy-start.20
  82.1 1.4 copy-start.21
  83.5 1.0 copy-start.22
  84.5 1.0 copy-start.24
  84.5 3.2 copy-start
  84.5 4.1 %copy-start.9 = (bf16[2,512,128]{2,1,0:T(8,128)(2,1)}, bf16[2,512,128]{2,1,0:T(8,128)(2,1)S(1)}, u32[]{:S(2)}) copy-start(bf16[2,512,128]{2,1,0:T(8,128)(2,1)S(1)} %get-tuple-element.43.eout_ref) | copy-start | bytes 786436
  88.9 8.8 %copy-start.18 = (s32[32]{0:T(128)}, s32[32]{0:T(128)S(1)}, u32[]{:S(2)}) copy-start(s32[32]{0:T(128)S(1)} %eq.15.order) | copy-start | bytes 388
  89.0 8.6 %copy-start.19 = (s32[32]{0:T(128)}, s32[32]{0:T(128)S(1)}, u32[]{:S(2)}) copy-start(s32[32]{0:T(128)S(1)} %select_reduce_fusion.src) | copy-start | bytes 388
  89.9 3.0 copy-start.30
  92.9 2.1 copy-start.28
  92.9 4.7 %copy-start.3 = (f32[2048,128]{1,0:T(8,128)S(1)}, f32[2048,128]{1,0:T(8,128)}, u32[]{:S(2)}) copy-start(f32[2048,128]{1,0:T(8,128)} %constant.26.clone.cos_ref) | copy-start | bytes 3145732
  92.9 4.7 %copy-start.4 = (f32[2048,128]{1,0:T(8,128)S(1)}, f32[2048,128]{1,0:T(8,128)}, u32[]{:S(2)}) copy-start(f32[2048,128]{1,0:T(8,128)} %constant.27.clone.sin_ref) | copy-start | bytes 3145732
  107.2 0.8 copy-start.8
  108.0 1.1 copy-start.23
  109.1 0.8 copy-start.25
  109.8 0.8 copy-start.26
  110.7 0.8 copy-start.27
  233.5 0.7 copy-start.34
  233.5 1.0 copy-start.29
  234.8 13.5 %copy-start.10 = (bf16[128,1024]{1,0:T(8,128)(2,1)S(1)}, bf16[128,1024]{1,0:T(8,128)(2,1)}, u32[]{:S(2)}) copy-start(bf16[128,1024]{1,0:T(8,128)(2,1)} %get-tuple-element.60.d_branch) | copy-start | bytes 786436
  234.8 13.5 %copy-start.11 = (bf16[128,1024]{1,0:T(8,128)(2,1)S(1)}, bf16[128,1024]{1,0:T(8,128)(2,1)}, u32[]{:S(2)}) copy-start(bf16[128,1024]{1,0:T(8,128)(2,1)} %get-tuple-element.62.hid_ref) | copy-start | bytes 786436
  234.8 13.5 %copy-start.13 = (bf16[128,128]{1,0:T(8,128)(2,1)S(1)}, bf16[128,128]{1,0:T(8,128)(2,1)}, u32[]{:S(2)}) copy-start(bf16[128,128]{1,0:T(8,128)(2,1)} %get-tuple-element.61.d_logits) | copy-start | bytes 98308
  248.3 1.3 copy-start.5
  249.5 62.5 %copy-start.32 = (f32[128,1024]{1,0:T(8,128)S(1)}, f32[128,1024]{1,0:T(8,128)}, u32[]{:S(2)}) copy-start(f32[128,1024]{1,0:T(8,128)} %get-tuple-element.52) | copy-start | bytes 1572868
  249.5 62.5 %copy-start.33 = (f32[128,1024]{1,0:T(8,128)S(1)}, f32[128,1024]{1,0:T(8,128)}, u32[]{:S(2)}) copy-start(f32[128,1024]{1,0:T(8,128)} %get-tuple-element.51) | copy-start | bytes 1572868
  249.5 64.1 %copy-start.2 = (bf16[128,1024]{1,0:T(8,128)(2,1)S(1)}, bf16[128,1024]{1,0:T(8,128)(2,1)}, u32[]{:S(2)}) copy-start(bf16[128,1024]{1,0:T(8,128)(2,1)} %x_ref.1) | copy-start | bytes 786436
  249.5 64.4 %copy-start.31 = (f32[128,1024]{1,0:T(8,128)S(1)}, f32[128,1024]{1,0:T(8,128)}, u32[]{:S(2)}) copy-start(f32[128,1024]{1,0:T(8,128)} %get-tuple-element.53) | copy-start | bytes 1572868
Sparse Core Ops, SparseCore 0:
  233.7 91.5 reduce-scatter.1
